TPU v7x, 32 devices: a whole 2x2x4 slice. The times are simulated.
32 devices in a mesh: bx: 8 (over z, x), by: 4 (over y, core).
Axes of the slice: x: 2, y: 2, z: 4, core: 2. Of those that a mesh axis runs over, the one named last changes fastest.
Arguments:
- features: bfloat16 [8, 4, 1024, 128], P('bx', 'by'), may hold values from -13 to 13
- live_count: int32 [8, 4], P('bx', 'by'), may hold values from 128 to 1024, as said below
- neighbour_map: int32 [8, 4, 27, 1024], P('bx', 'by'), may hold values from 0 to 2175, as said below
- send_rows: int32 [8, 4, 8, 128], P('bx', 'by'), may hold values from 0 to 1023, as said below
- weight: bfloat16 [3456, 128], replicated, may hold values from -0.109375 to 0.109375
- gain: float32 [128], replicated, may hold values from 0.5 to 1.5
- shift: float32 [128], replicated, may hold values from -3 to 3
- cotangent: bfloat16 [8, 4, 1024, 128], P('bx', 'by'), may hold values from -13 to 13
Outputs:
- activated: bfloat16 [8, 4, 1024, 128], P('bx', 'by')
- grad_features: bfloat16 [8, 4, 1024, 128], P('bx', 'by')
- grad_weight: float32 [27, 128, 128], P(None, 'bx', 'by')
Inputs may be any that keep to these rules, and one draw needn't show every extreme that they name: Rows 0 to live_count - 1 of a brick are live, the rest padding; in every draw some brick is full. `send_rows`: every entry is below its brick's live count; the eight blocks follow the directions (dx, dy) in row-major order with the brick's own position left out. `neighbour_map`: entries index the brick's extended table; offset 13 of a live row names that row itself; every entry of a padding row is 1536. With B = min(1024, 512) and q = r // B for a live row r, an entry below 1024 lies in rows q B to q B + B - 1, and an entry 1024 + b * 128 + h of incoming block b other than 4 has h in q * 128 B / 1024 to (q + 1) * 128 B / 1024 - 1.
All inputs are finite; a program needn't handle non-finite values.
Results may differ from a plain program's by a relative error of at most 0.029.
The roundings to bfloat16 on the way count: a program that leaves them out, or rounds other values in their place, can miss the bound.
Values may be sent and summed in bfloat16 or wider, within the bound.
A program may use at most 64 MiB of HBM per device.

v0:
```python
import jax
import jax.numpy as jnp
from jax import lax
from jax.sharding import PartitionSpec as P

epsilon = 1e-05


def extended(cells, sides, width):
    for axis, dim in sides:
        count = lax.axis_size(axis)
        ends = count - 1
        head = lax.slice_in_dim(cells, 0, width, axis=dim)
        tail = lax.slice_in_dim(cells, cells.shape[dim] - width, cells.shape[dim], axis=dim)
        cells = jnp.concatenate(
            [
                lax.ppermute(tail, axis, [(i, (i + 1) % count) for i in range(ends)]),
                cells,
                lax.ppermute(head, axis, [((i + 1) % count, i) for i in range(ends)]),
            ],
            axis=dim,
        )
    return cells


def from_neighbours(outgoing):
    padded = extended(outgoing, (("bx", 0), ("by", 1)), 1)
    return padded[::2, ::2]


def per_device(features, live_count, neighbour_map, send_rows, weight, gain, shift, cotangent):
    own_rows = features[0, 0]
    rows_total, channels = own_rows.shape
    halo_rows = send_rows.shape[3]
    block_rows = min(rows_total, 512)
    blocks_count = rows_total // block_rows
    halo_window = halo_rows // blocks_count
    window_rows = block_rows + 9 * halo_window
    sent_index = send_rows[0, 0].reshape(-1)
    send_select = (
        sent_index[:, None] == lax.broadcasted_iota(jnp.int32, (1, rows_total), 1)
    ).astype(jnp.bfloat16)
    chosen_rows = jnp.dot(send_select, own_rows, preferred_element_type=jnp.float32).astype(
        jnp.bfloat16
    )
    chosen_rows = chosen_rows.reshape(8, halo_rows, channels)
    blank_block = jnp.zeros((1, halo_rows, channels), jnp.bfloat16)
    outgoing = jnp.concatenate([chosen_rows[:4], blank_block, chosen_rows[4:]], axis=0).reshape(
        3, 3, halo_rows, channels
    )
    incoming = from_neighbours(outgoing).reshape(9, blocks_count, halo_window, channels)
    index_blocks = neighbour_map[0, 0].reshape(27, blocks_count, block_rows).transpose(1, 0, 2)
    own_blocks = own_rows.reshape(blocks_count, block_rows, channels)
    halo_blocks = incoming.transpose(1, 0, 2, 3)
    block_ids = jnp.arange(blocks_count, dtype=jnp.int32)

    def selector_of(indices, block_index):
        beyond = indices - rows_total
        target = beyond // halo_rows
        inside = beyond - target * halo_rows - block_index * halo_window
        local_pos = indices - block_index * block_rows
        remote_pos = block_rows + target * halo_window + inside
        usable = (inside >= 0) & (inside < halo_window)
        position = jnp.where(indices < rows_total, local_pos, jnp.where(usable, remote_pos, -1))
        return position[:, :, None] == lax.broadcasted_iota(jnp.int32, (1, 1, window_rows), 2)

    def forward_block(pieces):
        indices, own_part, halo_part, block_index = pieces
        window = jnp.concatenate([own_part, halo_part.reshape(9 * halo_window, channels)], axis=0)
        selector = selector_of(indices, block_index).astype(jnp.bfloat16)
        gathered = jnp.einsum(
            "kbw,wc->bkc", selector, window, preferred_element_type=jnp.float32
        ).astype(jnp.bfloat16)
        columns = gathered.reshape(block_rows, 27 * channels)
        return (jnp.dot(columns, weight, preferred_element_type=jnp.float32), columns)

    conv_blocks, column_blocks = lax.map(
        forward_block, (index_blocks, own_blocks, halo_blocks, block_ids)
    )
    conv_out = conv_blocks.reshape(rows_total, channels).astype(jnp.bfloat16)
    conv_float = conv_out.astype(jnp.float32)
    live_mask = (lax.broadcasted_iota(jnp.int32, (rows_total, 1), 0) < live_count[0, 0]).astype(
        jnp.float32
    )
    local_count = jnp.sum(live_mask)
    total_sum, total_count = lax.psum(
        (jnp.sum(conv_float * live_mask, axis=0), local_count), ("bx", "by")
    )
    center = total_sum / total_count
    deviation = (conv_float - center) * live_mask
    variance = lax.psum(jnp.sum(deviation * deviation, axis=0), ("bx", "by")) / total_count
    inverse_std = lax.rsqrt(variance + epsilon)
    normalized = (conv_float - center) * inverse_std
    before = gain * normalized + shift
    activated = (jnp.maximum(before, 0.0) * live_mask).astype(jnp.bfloat16)
    upstream = cotangent[0, 0].astype(jnp.float32) * (before > 0.0) * live_mask
    sum_up, sum_cross = lax.psum(
        (jnp.sum(upstream, axis=0), jnp.sum(upstream * normalized, axis=0)), ("bx", "by")
    )
    conv_grad = (
        gain
        * inverse_std
        * (upstream - live_mask * (sum_up + normalized * sum_cross) / total_count)
    ).astype(jnp.bfloat16)
    grad_blocks = conv_grad.reshape(blocks_count, block_rows, channels)

    def backward_block(weight_acc, pieces):
        indices, columns, grad_rows, block_index = pieces
        weight_acc = weight_acc + lax.dot_general(
            columns, grad_rows, (((0,), (0,)), ((), ())), preferred_element_type=jnp.float32
        )
        column_grad = lax.dot_general(
            grad_rows, weight, (((1,), (1,)), ((), ())), preferred_element_type=jnp.float32
        )
        column_grad = column_grad.reshape(block_rows, 27, channels)
        selector = selector_of(indices, block_index).astype(jnp.float32)
        window_grad = jnp.einsum(
            "kbw,bkc->wc",
            selector,
            column_grad,
            precision=lax.Precision.HIGHEST,
            preferred_element_type=jnp.float32,
        )
        return (
            weight_acc,
            (window_grad[:block_rows], window_grad[block_rows:].reshape(9, halo_window, channels)),
        )

    start_acc = jnp.zeros((27 * channels, channels), jnp.float32)
    weight_acc, (own_parts, halo_parts) = lax.scan(
        backward_block, start_acc, (index_blocks, column_blocks, grad_blocks, block_ids)
    )
    weight_terms = weight_acc.reshape(27, channels, channels)
    partial_x = lax.psum_scatter(
        weight_terms.astype(jnp.bfloat16), "bx", scatter_dimension=1, tiled=True
    )
    summed = lax.psum_scatter(partial_x, "by", scatter_dimension=2, tiled=True).astype(jnp.float32)
    grad_weight = summed / jnp.sqrt(total_count)
    own_table = own_parts.reshape(rows_total, channels)
    halo_table = halo_parts.transpose(1, 0, 2, 3).reshape(3, 3, halo_rows, channels)
    halo_grad = halo_table.astype(jnp.bfloat16)
    returned = from_neighbours(halo_grad).reshape(9, halo_rows, channels)
    slots_back = (
        jnp.concatenate([returned[:4], returned[5:]], axis=0)
        .reshape(-1, channels)
        .astype(jnp.float32)
    )
    added_back = lax.dot_general(
        send_select.astype(jnp.float32),
        slots_back,
        (((0,), (0,)), ((), ())),
        precision=lax.Precision.HIGHEST,
        preferred_element_type=jnp.float32,
    )
    own_grad = own_table + added_back
    return (activated[None, None], own_grad.astype(jnp.bfloat16)[None, None], grad_weight)


def solution(mesh):
    return jax.shard_map(
        per_device,
        mesh=mesh,
        in_specs=(
            P("bx", "by", None, None),
            P("bx", "by"),
            P("bx", "by", None, None),
            P("bx", "by", None, None),
            P(),
            P(),
            P(),
            P("bx", "by", None, None),
        ),
        out_specs=(P("bx", "by", None, None), P("bx", "by", None, None), P(None, "bx", "by")),
        check_vma=False,
    )
```

profile of v0, /device:TPU:0, one launch (start us, length us, event | category | flops | bytes accessed | tf_op | source)
XLA Modules:
  0.0 364.1 jit_solution(10704451228064157090)
XLA Ops:
  9.1 4.8 %collective-permute-start = (bf16[1,3,128,128]{3,2,1,0:T(8,128)(2,1)S(1)}, bf16[1,3,128,128]{3,2,1,0:T(8,128)(2,1)S(1)}, u32[]{:S(2)}, u32[]{:S(2)}) collective-permute-start(bf16[1,3,128,128]{3,2,1,0:T(8,128)(2,1)S(1)} %bitcast.238), channel_id=1, source_target_pairs={{0,4},{4,8},{8,12},{12,16},{16,20},{20,24},{24,28},{1,5},{5,9},{9,... | collective-permute-start | bytes 294920 | tf_op jit(solution)/shard_map/ppermute | solution.py:17
  16.2 4.3 %collective-permute-done.1 = bf16[1,3,128,128]{3,2,1,0:T(8,128)(2,1)S(1)} collective-permute-done((bf16[1,3,128,128]{3,2,1,0:T(8,128)(2,1)S(1)}, bf16[1,3,128,128]{3,2,1,0:T(8,128)(2,1)S(1)}, u32[]{:S(2)}, u32[]{:S(2)}) %collective-permute-start.1) | collective-permute-done | bytes 98336 | tf_op jit(solution)/shard_map/ppermute | solution.py:19
  21.2 1.9 collective-permute-start.2
  29.1 38.2 %while.33 = (s32[]{:T(128)}, bf16[2,512,128]{2,1,0:T(8,128)(2,1)S(1)}, bf16[2,512,3456]{1,2,0:T(8,128)(2,1)}, bf16[2,512,128]{2,1,0:T(8,128)(2,1)}, bf16[2,9,64,...) while((s32[]{:T(128)}, ...), condition=%wide.region_1.2_spmd.clone, body=%wide.region_0.1_spmd.sunk.clone | while | flops 4321123840 | bytes 16304801 | solution.py:77
  32.0 13.0 %fusion.82 = bf16[128,27,512]{2,0,1:T(8,128)(2,1)S(1)} fusion(s32[27,512]{1,0:T(8,128)S(1)} %bitcast_select_fusion.6, bf16[576,128]{1,0:T(8,128)(2,1)S(1)} %bitcast.223, bf16[512,128]{1,0:T(8,128)(2,1)S(1)} %dynamic-slice_bitcast_fusion.3), kind=kOutput, calls=%fused_computation.3.clone.1.clone | convolution fusion | flops 3867738112 | bytes 3872768 | tf_op jit(solution)/shard_map/while/body/eval_jaxpr/kbw,wc->bkc/dot_general | solution.py:71
  45.0 2.0 constant_dynamic-update-slice_fusion.6
  51.1 13.0 %fusion.82 = bf16[128,27,512]{2,0,1:T(8,128)(2,1)S(1)} fusion(s32[27,512]{1,0:T(8,128)S(1)} %bitcast_select_fusion.6, bf16[576,128]{1,0:T(8,128)(2,1)S(1)} %bitcast.223, bf16[512,128]{1,0:T(8,128)(2,1)S(1)} %dynamic-slice_bitcast_fusion.3), kind=kOutput, calls=%fused_computation.3.clone.1.clone | convolution fusion | flops 3867738112 | bytes 3872768 | tf_op jit(solution)/shard_map/while/body/eval_jaxpr/kbw,wc->bkc/dot_general | solution.py:71
  64.1 2.0 constant_dynamic-update-slice_fusion.6
  67.5 43.9 %all-reduce.1 = (f32[128]{0:T(128)S(1)}, f32[]{:T(128)}) all-reduce(f32[128]{0:T(128)S(1)} %multiply_reduce_fusion.1, f32[]{:T(128)} %fusion.44), channel_id=1, replica_groups=mesh['bx'=8,'by'=4] {'bx','by'}, use_global_device_ids=true, to_apply=%region_3.4 | all-reduce | flops 129 | bytes 1032 | tf_op jit(solution)/shard_map/psum | solution.py:86
  112.3 39.3 %psum.37 = f32[128]{0:T(128)S(1)} all-reduce(f32[128]{0:T(128)S(1)} %multiply_reduce_fusion), channel_id=1, replica_groups=mesh['bx'=8,'by'=4] {'bx','by'}, use_global_device_ids=true, to_apply=%region_7.8 | all-reduce | flops 128 | bytes 1024 | tf_op jit(solution)/shard_map/psum | solution.py:91
  153.5 41.1 %all-reduce = (f32[128]{0:T(128)S(1)}, f32[128]{0:T(128)S(1)}) all-reduce(f32[128]{0:T(128)S(1)} %get-tuple-element.320, f32[128]{0:T(128)S(1)} %get-tuple-element.319), channel_id=1, replica_groups=mesh['bx'=8,'by'=4] {'bx','by'}, use_global_device_ids=true, to_apply=%region_11.12 | all-reduce | flops 256 | bytes 2048 | tf_op jit(solution)/shard_map/psum | solution.py:97
  196.6 73.1 %while.34 = (s32[]{:T(128)}, f32[3456,128]{1,0:T(8,128)S(1)}, f32[2,512,128]{2,1,0:T(8,128)}, bf16[2,9,64,128]{3,2,0,1:T(8,128)(2,1)}, bf16[2,512,3456]{1,2,0:T(...) while((s32[]{:T(128)}, f32[3456,128]{1,0:T(8,128)S(1)}, ...), condition=%wide.region_13.14_spmd.clone.clone, body=%wide.region_12.13_spmd.clone.sunk.clone | while | flops 24024522752 | bytes 28413672 | solution.py:130
  199.6 28.7 %fusion.90 = f32[1088,128]{1,0:T(8,128)S(1)} fusion(f32[512,27,128]{2,0,1:T(8,128)S(1)} %fusion.89, s32[27,512]{1,0:T(8,128)S(1)} %bitcast_select_fusion.7), kind=kOutput, calls=%fused_computation.31.clone.1.clone | convolution fusion | flops 23117266944 | bytes 7690240 | tf_op jit(solution)/shard_map/while/body/eval_jaxpr/kbw,bkc->wc/dot_general | solution.py:117
  229.9 3.2 convolution_add_fusion.3
  236.2 28.7 %fusion.90 = f32[1088,128]{1,0:T(8,128)S(1)} fusion(f32[512,27,128]{2,0,1:T(8,128)S(1)} %fusion.89, s32[27,512]{1,0:T(8,128)S(1)} %bitcast_select_fusion.7), kind=kOutput, calls=%fused_computation.31.clone.1.clone | convolution fusion | flops 23117266944 | bytes 7690240 | tf_op jit(solution)/shard_map/while/body/eval_jaxpr/kbw,bkc->wc/dot_general | solution.py:117
  266.4 3.2 convolution_add_fusion.3
  271.8 4.2 %collective-permute-start.4 = (bf16[1,3,128,128]{3,2,1,0:T(8,128)(2,1)S(1)}, bf16[1,3,128,128]{3,2,1,0:T(8,128)(2,1)S(1)}, u32[]{:S(2)}, u32[]{:S(2)}) collective-permute-start(bf16[1,3,128,128]{3,2,1,0:T(8,128)(2,1)S(1)} %bitcast.240), channel_id=1, source_target_pairs={{0,4},{4,8},{8,12},{12,16},{16,20},{20,24},{24,28},{1,5},{5,9},{9,... | collective-permute-start | bytes 294920 | tf_op jit(solution)/shard_map/ppermute | solution.py:17
  278.0 2.6 collective-permute-done.4
  287.2 2.1 collective-permute-done.7
  290.5 41.6 %reduce-scatter.5.cloned.1.call-done = bf16[27,16,128]{2,1,0:T(8,128)(2,1)} async-done(((bf16[27,128,128]{2,1,0:T(8,128)(2,1)}), bf16[27,16,128]{2,1,0:T(8,128)(2,1)}) %reduce-scatter.5.cloned.1.call-update) | async-done | bytes 110608 | tf_op jit(solution)/shard_map/reduce_scatter | solution.py:134
  332.1 2.3 copy.27
  334.4 2.1 reshape.445
  336.6 2.2 fusion.35
  338.8 16.5 %reduce-scatter.7.cloned.1.call-done = bf16[32,432]{1,0:T(8,128)(2,1)} async-done(((bf16[128,432]{1,0:T(8,128)(2,1)}), bf16[32,432]{1,0:T(8,128)(2,1)}) %reduce-scatter.7.cloned.1.call-update) | async-done | bytes 27664
  (92 shorter events, 40.0 us)
Async XLA Ops:
  7.2 21.9 %copy-start = (bf16[3456,128]{1,0:T(8,128)(2,1)S(1)}, bf16[3456,128]{1,0:T(8,128)(2,1)}, u32[]{:S(2)}) copy-start(bf16[3456,128]{1,0:T(8,128)(2,1)} %param.16) | copy-start | bytes 2654212
  7.2 324.9 %reduce-scatter.5.cloned.1.call-start = ((), (), s32[]{:S(2)}) async-start(), calls=%async_computation.2 | async-start | bytes 995328 | tf_op jit(solution)/shard_map/reduce_scatter | solution.py:134
  9.1 7.0 %collective-permute-start = (bf16[1,3,128,128]{3,2,1,0:T(8,128)(2,1)S(1)}, bf16[1,3,128,128]{3,2,1,0:T(8,128)(2,1)S(1)}, u32[]{:S(2)}, u32[]{:S(2)}) collective-permute-start(bf16[1,3,128,128]{3,2,1,0:T(8,128)(2,1)S(1)} %bitcast.238), channel_id=1, source_target_pairs={{0,4},{4,8},{8,12},{12,16},{16,20},{20,24},{24,28},{1,5},{5,9},{9,... | collective-permute-start | bytes 294920 | tf_op jit(solution)/shard_map/ppermute | solution.py:17
  14.0 6.5 %collective-permute-start.1 = (bf16[1,3,128,128]{3,2,1,0:T(8,128)(2,1)S(1)}, bf16[1,3,128,128]{3,2,1,0:T(8,128)(2,1)S(1)}, u32[]{:S(2)}, u32[]{:S(2)}) collective-permute-start(bf16[1,3,128,128]{3,2,1,0:T(8,128)(2,1)S(1)} %bitcast.237), channel_id=1, source_target_pairs={{4,0},{8,4},{12,8},{16,12},{20,16},{24,20},{28,24},{5,1},{9,5},{13... | collective-permute-start | bytes 294920 | tf_op jit(solution)/shard_map/ppermute | solution.py:19
  21.2 5.2 %collective-permute-start.2 = (bf16[5,1,128,128]{3,2,1,0:T(8,128)(2,1)}, bf16[5,1,128,128]{3,2,1,0:T(8,128)(2,1)}, u32[]{:S(2)}, u32[]{:S(2)}) collective-permute-start(bf16[5,1,128,128]{3,2,1,0:T(8,128)(2,1)} %get-tuple-element.363), channel_id=1, source_target_pairs={{0,1},{1,2},{2,3},{4,5},{5,6},{6,7},{8,9},{9,10},{10,11},{12,13},{... | collective-permute-start | bytes 491528 | tf_op jit(solution)/shard_map/ppermute | solution.py:17
  23.2 4.7 %collective-permute-start.3 = (bf16[5,1,128,128]{3,2,1,0:T(8,128)(2,1)}, bf16[5,1,128,128]{3,2,1,0:T(8,128)(2,1)}, u32[]{:S(2)}, u32[]{:S(2)}) collective-permute-start(bf16[5,1,128,128]{3,2,1,0:T(8,128)(2,1)} %get-tuple-element.364), channel_id=1, source_target_pairs={{1,0},{2,1},{3,2},{5,4},{6,5},{7,6},{9,8},{10,9},{11,10},{13,12},{... | collective-permute-start | bytes 491528 | tf_op jit(solution)/shard_map/ppermute | solution.py:19
  29.1 122.6 %copy-start.1 = (f32[128]{0:T(128)S(1)}, f32[128]{0:T(128)}, u32[]{:S(2)}) copy-start(f32[128]{0:T(128)} %param.17) | copy-start | bytes 1540
  29.1 123.2 %copy-start.2 = (f32[128]{0:T(128)S(1)}, f32[128]{0:T(128)}, u32[]{:S(2)}) copy-start(f32[128]{0:T(128)} %param.18) | copy-start | bytes 1540
  199.6 28.7 %copy-start.3 = (f32[2,512,128]{2,1,0:T(8,128)S(1)}, f32[2,512,128]{2,1,0:T(8,128)}, u32[]{:S(2)}) copy-start(f32[2,512,128]{2,1,0:T(8,128)} %get-tuple-element.571) | copy-start | bytes 1572868 | tf_op jit(solution)/shard_map/while
  228.4 0.8 copy-start.4
  236.2 28.7 %copy-start.3 = (f32[2,512,128]{2,1,0:T(8,128)S(1)}, f32[2,512,128]{2,1,0:T(8,128)}, u32[]{:S(2)}) copy-start(f32[2,512,128]{2,1,0:T(8,128)} %get-tuple-element.571) | copy-start | bytes 1572868 | tf_op jit(solution)/shard_map/while
  265.0 0.8 copy-start.4
  269.7 66.9 %copy-start.6 = (s32[1,1,8,128]{3,2,1,0:T(8,128)S(1)}, s32[1,1,8,128]{3,2,1,0:T(8,128)}, u32[]{:S(2)}) copy-start(s32[1,1,8,128]{3,2,1,0:T(8,128)} %param.15) | copy-start | bytes 12292
  270.7 65.9 %copy-start.5 = (f32[2,512,128]{2,1,0:T(8,128)S(1)}, f32[2,512,128]{2,1,0:T(8,128)}, u32[]{:S(2)}) copy-start(f32[2,512,128]{2,1,0:T(8,128)} %get-tuple-element.226) | copy-start | bytes 1572868
  270.7 84.5 %reduce-scatter.7.cloned.1.call-start = ((), (), s32[]{:S(2)}) async-start(), calls=%async_computation.3 | async-start | bytes 163840
  271.8 8.8 %collective-permute-start.4 = (bf16[1,3,128,128]{3,2,1,0:T(8,128)(2,1)S(1)}, bf16[1,3,128,128]{3,2,1,0:T(8,128)(2,1)S(1)}, u32[]{:S(2)}, u32[]{:S(2)}) collective-permute-start(bf16[1,3,128,128]{3,2,1,0:T(8,128)(2,1)S(1)} %bitcast.240), channel_id=1, source_target_pairs={{0,4},{4,8},{8,12},{12,16},{16,20},{20,24},{24,28},{1,5},{5,9},{9,... | collective-permute-start | bytes 294920 | tf_op jit(solution)/shard_map/ppermute | solution.py:17
  276.0 6.5 %collective-permute-start.5 = (bf16[1,3,128,128]{3,2,1,0:T(8,128)(2,1)S(1)}, bf16[1,3,128,128]{3,2,1,0:T(8,128)(2,1)S(1)}, u32[]{:S(2)}, u32[]{:S(2)}) collective-permute-start(bf16[1,3,128,128]{3,2,1,0:T(8,128)(2,1)S(1)} %bitcast.239), channel_id=1, source_target_pairs={{4,0},{8,4},{12,8},{16,12},{20,16},{24,20},{28,24},{5,1},{9,5},{13... | collective-permute-start | bytes 294920 | tf_op jit(solution)/shard_map/ppermute | solution.py:19
  283.5 3.7 %collective-permute-start.6 = (bf16[5,1,128,128]{3,2,1,0:T(8,128)(2,1)S(1)}, bf16[5,1,128,128]{3,2,1,0:T(8,128)(2,1)S(1)}, u32[]{:S(2)}, u32[]{:S(2)}) collective-permute-start(bf16[5,1,128,128]{3,2,1,0:T(8,128)(2,1)S(1)} %get-tuple-element.361), channel_id=1, source_target_pairs={{0,1},{1,2},{2,3},{4,5},{5,6},{6,7},{8,9},{9,10},{10,11},{12,13},{... | collective-permute-start | bytes 491528 | tf_op jit(solution)/shard_map/ppermute | solution.py:17
  284.8 4.5 %collective-permute-start.7 = (bf16[5,1,128,128]{3,2,1,0:T(8,128)(2,1)S(1)}, bf16[5,1,128,128]{3,2,1,0:T(8,128)(2,1)S(1)}, u32[]{:S(2)}, u32[]{:S(2)}) collective-permute-start(bf16[5,1,128,128]{3,2,1,0:T(8,128)(2,1)S(1)} %get-tuple-element.362), channel_id=1, source_target_pairs={{1,0},{2,1},{3,2},{5,4},{6,5},{7,6},{9,8},{10,9},{11,10},{13,12},{... | collective-permute-start | bytes 491528 | tf_op jit(solution)/shard_map/ppermute | solution.py:19
Sparse Core Ops, SparseCore 0:
  270.9 61.1 reduce-scatter.4
  336.7 18.5 reduce-scatter.6
where the time goes:
time: 365 us; the launch traced here: 364 us
  blocking collectives  124 us (34%)
  matrix products  98.4 us (27%)
  waiting for transfers between devices  70.5 us (19%)
  local copies, waits for them, and re-layouts  18.3 us (5%)
  starting transfers between devices  17.7 us (5%)
  between operations  15.7 us (4%)
  other arithmetic  13.6 us (4%)
  loops' own time  5.44 us (1%)
    dot_general x2, matrix products, backward_block(): jnp.einsum('kbw,bkc->wc', selector, column_grad, precision=lax.Precision....  57.4 us
    psum x1, blocking collectives, per_device(): lax.psum((jnp.sum(conv_float * live_mask, axis=0), local_count), ('bx', '...  43.9 us
    reduce_scatter x1, waiting for transfers between devices, per_device(): lax.psum_scatter(weight_terms.astype(jnp.bfloat16), 'bx', scatter_dimensi...  41.6 us
    psum x1, blocking collectives, per_device(): lax.psum((jnp.sum(upstream, axis=0), jnp.sum(upstream * normalized, axis=...  41.1 us
    psum x1, blocking collectives, per_device(): lax.psum(jnp.sum(deviation * deviation, axis=0), ('bx', 'by')) / total_count  39.3 us
    dot_general x2, matrix products, forward_block(): jnp.einsum('kbw,wc->bkc', selector, window, preferred_element_type=jnp.fl...  25.9 us
    unnamed x3, waiting for transfers between devices  16.5 us
    ppermute x4, starting transfers between devices, extended(): lax.ppermute(tail, axis, [(i, (i + 1) % count) for i in range(ends)])  12.3 us
  transfers between devices with their start and end apart: 10, of which 7 were waited for; matrix products, arithmetic and copies ran while one was open for 2% of the time, Pallas kernels for 0%

commit v1 on v0

v1 whole, which is shorter than its diff:
```python
import functools

import jax
import jax.numpy as jnp
from jax import lax
from jax.experimental import pallas as pl
from jax.experimental.pallas import tpu as pltpu
from jax.sharding import PartitionSpec as P

epsilon = 1e-05
OFFSETS = 27
GROUP = 3
MESH = pl.DeviceIdType.MESH
f32 = jnp.float32
bf16 = jnp.bfloat16


def one_hot(mask):
    return jnp.where(mask, 1.0, 0.0).astype(bf16)


def lanes_from_row(row):
    return jnp.broadcast_to(row, (128, row.shape[1])).T


def row_selector(row, width):
    wide = lanes_from_row(row)
    lane = lax.broadcasted_iota(jnp.int32, wide.shape, 1)
    return jnp.concatenate([one_hot(wide == lane + j) for j in range(0, width, 128)], axis=1)


def kernel(
    nx, ny, live_ref, feat, nmap, send, weight, gain, shift, cot,
    act_out, gf_out, gw_out,
    outgoing, incoming, code, table, cols, conv, grad, acc, own_tab, hbuf, returned,
    stat_y, stat_x, part, part_in, piece, piece_in,
    h_send, h_recv, sy_send, sy_recv, sx_send, sx_recv, r_send, r_recv,
    wy_send, wy_recv, wx_send, wx_recv,
):
    x, y = lax.axis_index("bx"), lax.axis_index("by")
    rows, channels = feat.shape
    block = rows // 2
    window = send.shape[1] // 2
    slice_y = channels // ny
    slice_x = channels // nx
    groups = piece.shape[1]
    directions = [(i - 1, j - 1) for i in range(3) for j in range(3) if (i, j) != (1, 1)]

    def exists(dx, dy):
        ok = None
        for cond in (
            [x > 0] if dx < 0 else [x < nx - 1] if dx > 0 else []
        ) + ([y > 0] if dy < 0 else [y < ny - 1] if dy > 0 else []):
            ok = cond if ok is None else jnp.logical_and(ok, cond)
        return ok

    def near(dx, dy):
        return (x + dx, y + dy)

    barrier = pltpu.get_barrier_semaphore()
    for d in range(1, ny):
        pl.semaphore_signal(barrier, inc=1, device_id=(x, lax.rem(y + d, ny)), device_id_type=MESH)
    for d in range(1, nx):
        pl.semaphore_signal(barrier, inc=1, device_id=(lax.rem(x + d, nx), y), device_id_type=MESH)
    diagonals = [(dx, dy) for dx, dy in directions if dx and dy]
    for dx, dy in diagonals:
        @pl.when(exists(dx, dy))
        def _(dx=dx, dy=dy):
            pl.semaphore_signal(barrier, inc=1, device_id=near(dx, dy), device_id_type=MESH)

    for s in range(8):
        chosen = jnp.dot(
            row_selector(send[s : s + 1, :], rows), feat[...], preferred_element_type=f32
        ).astype(bf16)
        outgoing[0, s] = chosen[:window]
        outgoing[1, s] = chosen[window:]

    beside_x = (x + nx - 1) // nx + (2 * nx - 2 - x) // nx
    beside_y = (y + ny - 1) // ny + (2 * ny - 2 - y) // ny
    pl.semaphore_wait(barrier, nx + ny - 2 + beside_x * beside_y)

    def halo_copy(s):
        return pltpu.make_async_remote_copy(
            src_ref=outgoing.at[:, s],
            dst_ref=incoming.at[:, 7 - s],
            send_sem=h_send.at[s],
            recv_sem=h_recv.at[7 - s],
            device_id=near(*directions[s]),
            device_id_type=MESH,
        )

    def halo_arrival(s):
        return pltpu.make_async_remote_copy(
            src_ref=outgoing.at[:, s],
            dst_ref=incoming.at[:, s],
            send_sem=h_send.at[s],
            recv_sem=h_recv.at[s],
            device_id=near(*directions[s]),
            device_id_type=MESH,
        )

    for s, (dx, dy) in enumerate(directions):
        @pl.when(exists(dx, dy))
        def _(s=s):
            halo_copy(s).start()

        @pl.when(jnp.logical_not(exists(dx, dy)))
        def _(s=s):
            incoming[:, s] = jnp.zeros((2, window, channels), bf16)
            returned[s] = jnp.zeros((2 * window, channels), bf16)

    entry = nmap[...]
    beyond = entry - rows
    target = beyond // (2 * window)
    inside = lax.rem(beyond, 2 * window)
    inside = jnp.where(inside >= window, inside - window, inside)
    slot = jnp.where(target > 4, target - 1, target)
    far = jnp.where(target == 4, 1023, 1024 + slot * window + inside)
    own = jnp.where(entry >= block, entry - block, entry)
    code[0:OFFSETS, :] = jnp.where(entry < rows, own, far)

    for q in range(2):
        table[q, :, 0:channels] = feat[q * block : (q + 1) * block, :]
    for s, (dx, dy) in enumerate(directions):
        @pl.when(exists(dx, dy))
        def _(s=s):
            halo_arrival(s).wait_recv()
    for q in range(2):
        table[q, :, channels:] = incoming[q].reshape(block, channels)

    for q in range(2):
        lo = q * block

        def gather(g, carry):
            for j in range(GROUP):
                k = g * GROUP + j
                row = code[pl.ds(k, 1), lo : lo + block]
                wide = lanes_from_row(row)
                low = jnp.bitwise_and(wide, 1023)
                lane = lax.broadcasted_iota(jnp.int32, wide.shape, 1)
                pick = jnp.concatenate(
                    [one_hot(low == lane + t) for t in range(0, block, 128)], axis=1
                )
                both = jnp.dot(pick, table[q], preferred_element_type=f32)
                got = jnp.where(wide >= 1024, both[:, channels:], both[:, :channels])
                cols[lo : lo + block, pl.ds(pl.multiple_of(k * 128, 128), 128)] = got.astype(bf16)
            return carry

        lax.fori_loop(0, OFFSETS // GROUP, gather, 0)
        conv[lo : lo + block, :] = jnp.dot(
            cols[lo : lo + block, :], weight[...], preferred_element_type=f32
        ).astype(bf16)

    def spread(buf, r, me, count, peer, send_sems, recv_sems):
        def copy(d, arriving):
            other = lax.rem(me + d, count)
            place = other if arriving else me
            return pltpu.make_async_remote_copy(
                src_ref=buf.at[r, me],
                dst_ref=buf.at[r, place],
                send_sem=send_sems.at[r, other],
                recv_sem=recv_sems.at[r, place],
                device_id=peer(other),
                device_id_type=MESH,
            )

        for d in range(1, count):
            copy(d, False).start()
        for d in range(1, count):
            copy(d, True).wait_recv()
        for d in range(1, count):
            copy(d, False).wait_send()

    def pooled(buf, r, count):
        items = [buf[r, i] for i in range(count)]
        n = functools.reduce(jnp.add, [v[0:1] for v in items])
        s = functools.reduce(jnp.add, [v[1:2] for v in items])
        mean = s / n
        m2 = jnp.zeros_like(s)
        for v in items:
            dev = v[1:2] / v[0:1] - mean
            m2 = m2 + (v[2:3] + v[0:1] * dev * dev)
        return n, s, m2

    along_y = lambda other: (x, other)
    along_x = lambda other: (other, y)

    def put(buf, r, me, *vectors):
        pad = jnp.zeros((8 - len(vectors), channels), f32)
        buf[r, me] = jnp.concatenate(list(vectors) + [pad], axis=0)

    live_rows = live_ref[0, 0]
    live = jnp.where(
        lax.broadcasted_iota(jnp.int32, (rows, channels), 0) < live_rows, 1.0, 0.0
    ).astype(f32)
    values = conv[...].astype(f32)
    n_own = jnp.full((1, channels), live_rows, jnp.int32).astype(f32)
    s_own = jnp.sum(values * live, axis=0, keepdims=True)
    dev = (values - s_own / n_own) * live
    m2_own = jnp.sum(dev * dev, axis=0, keepdims=True)
    put(stat_y, 0, y, n_own, s_own, m2_own)
    spread(stat_y, 0, y, ny, along_y, sy_send, sy_recv)
    put(stat_x, 0, x, *pooled(stat_y, 0, ny))
    spread(stat_x, 0, x, nx, along_x, sx_send, sx_recv)
    total, s_all, m2_all = pooled(stat_x, 0, nx)
    center = s_all / total
    inverse = lax.rsqrt(m2_all / total + epsilon)

    normalized = (values - center) * inverse
    before = gain[...] * normalized + shift[...]
    act_out[...] = (jnp.maximum(before, 0.0) * live).astype(bf16)
    upstream = jnp.where(before > 0.0, cot[...].astype(f32), 0.0) * live
    put(
        stat_y, 1, y,
        jnp.sum(upstream, axis=0, keepdims=True),
        jnp.sum(upstream * normalized, axis=0, keepdims=True),
    )
    spread(stat_y, 1, y, ny, along_y, sy_send, sy_recv)
    stat_x[1, x] = functools.reduce(jnp.add, [stat_y[1, i] for i in range(ny)])
    spread(stat_x, 1, x, nx, along_x, sx_send, sx_recv)
    sums = functools.reduce(jnp.add, [stat_x[1, i] for i in range(nx)])
    sum_up, sum_cross = sums[0:1], sums[1:2]
    conv_grad = (
        gain[...] * inverse * (upstream - live * (sum_up + normalized * sum_cross) / total)
    ).astype(bf16)
    grad[...] = conv_grad

    flipped = conv_grad.astype(f32).T.astype(bf16)
    wide_part = GROUP * 128

    def weight_part(g, carry):
        at = pl.ds(pl.multiple_of(g * wide_part, 128), wide_part)
        term = jnp.dot(flipped, cols[:, at], preferred_element_type=f32).astype(bf16)
        part[:, :, at] = term.reshape(ny, slice_y, wide_part)
        return carry

    lax.fori_loop(0, OFFSETS // GROUP, weight_part, 0)

    def part_copy(d, arriving):
        other = lax.rem(y + d, ny)
        place = other if arriving else y
        return pltpu.make_async_remote_copy(
            src_ref=part.at[other],
            dst_ref=part_in.at[place],
            send_sem=wy_send.at[other],
            recv_sem=wy_recv.at[place],
            device_id=(x, other),
            device_id_type=MESH,
        )

    for d in range(1, ny):
        part_copy(d, False).start()

    def scatter(q):
        lo = q * block
        acc[...] = jnp.zeros_like(acc)

        def step(g, carry):
            at = pl.ds(pl.multiple_of(g * wide_part, 128), wide_part)
            col_grad = lax.dot_general(
                grad[lo : lo + block, :], weight[at, :], (((1,), (1,)), ((), ())),
                preferred_element_type=f32,
            )
            picks, terms = [], []
            place = lax.broadcasted_iota(jnp.int32, (block, block), 0)
            for j in range(GROUP):
                row = code[pl.ds(g * GROUP + j, 1), lo : lo + block]
                picks.append(one_hot(place == jnp.bitwise_and(row, 1023)))
                away = lanes_from_row(row) >= 1024
                term = col_grad[:, j * 128 : (j + 1) * 128]
                terms.append(
                    jnp.concatenate(
                        [jnp.where(away, 0.0, term), jnp.where(away, term, 0.0)], axis=1
                    ).astype(bf16)
                )
            acc[...] += jnp.dot(
                jnp.concatenate(picks, axis=1),
                jnp.concatenate(terms, axis=0),
                preferred_element_type=f32,
            )
            return carry

        lax.fori_loop(0, OFFSETS // GROUP, step, 0)
        own_tab[lo : lo + block, :] = acc[:, 0:channels]
        hbuf[q] = acc[:, channels:].astype(bf16).reshape(8, window, channels)

    def back_copy(q, s, arriving):
        to = s if arriving else 7 - s
        return pltpu.make_async_remote_copy(
            src_ref=hbuf.at[q, s],
            dst_ref=returned.at[to, pl.ds(q * window, window)],
            send_sem=r_send.at[q, s],
            recv_sem=r_recv.at[q, to],
            device_id=near(*directions[s]),
            device_id_type=MESH,
        )

    def send_back(q):
        for s, (dx, dy) in enumerate(directions):
            @pl.when(exists(dx, dy))
            def _(s=s):
                back_copy(q, s, False).start()

    scatter(0)
    send_back(0)

    part_in[y] = part[y]
    for d in range(1, ny):
        part_copy(d, True).wait_recv()
    for g in range(groups):
        strips = []
        for j in range(ny):
            k = g * ny + j
            if k < OFFSETS:
                strip = part_in[:, :, k * 128 : (k + 1) * 128].astype(f32)
                strips.append(jnp.sum(strip, axis=0))
            else:
                strips.append(jnp.zeros((slice_y, 128), f32))
        turned = jnp.concatenate(strips, axis=0).T
        piece[:, g] = turned.reshape(nx, slice_x, channels).astype(bf16)

    def piece_copy(d, arriving):
        other = lax.rem(x + d, nx)
        place = other if arriving else x
        return pltpu.make_async_remote_copy(
            src_ref=piece.at[other],
            dst_ref=piece_in.at[place],
            send_sem=wx_send.at[other],
            recv_sem=wx_recv.at[place],
            device_id=(other, y),
            device_id_type=MESH,
        )

    for d in range(1, nx):
        piece_copy(d, False).start()

    scatter(1)
    send_back(1)

    piece_in[x] = piece[x]
    for d in range(1, nx):
        piece_copy(d, True).wait_recv()
    scale = 1.0 / jnp.sqrt(total)
    for g in range(groups):
        summed = jnp.sum(piece_in[:, g].astype(f32), axis=0) * scale
        for j in range(ny):
            if g * ny + j < OFFSETS:
                gw_out[g * ny + j] = summed[:, j * slice_y : (j + 1) * slice_y]

    for q in range(2):
        for s, (dx, dy) in enumerate(directions):
            @pl.when(exists(dx, dy))
            def _(q=q, s=s):
                back_copy(q, s, True).wait_recv()
    place = lax.broadcasted_iota(jnp.int32, (rows, 2 * window), 0)
    pick = jnp.concatenate([one_hot(place == send[s : s + 1, :]) for s in range(8)], axis=1)
    added = jnp.dot(
        pick, returned[...].reshape(8 * 2 * window, channels), preferred_element_type=f32
    )
    gf_out[...] = (own_tab[...] + added).astype(bf16)

    for s, (dx, dy) in enumerate(directions):
        @pl.when(exists(dx, dy))
        def _(s=s):
            halo_copy(s).wait_send()
            for q in range(2):
                back_copy(q, s, False).wait_send()
    for d in range(1, ny):
        part_copy(d, False).wait_send()
    for d in range(1, nx):
        piece_copy(d, False).wait_send()


def per_device(features, live_count, neighbour_map, send_rows, weight, gain, shift, cotangent):
    nx, ny = lax.axis_size("bx"), lax.axis_size("by")
    rows, channels = features.shape[2:]
    halo = send_rows.shape[3]
    block, window = rows // 2, halo // 2
    slice_x, slice_y = channels // nx, channels // ny
    groups = -(-OFFSETS // ny)
    vmem = pl.BlockSpec(memory_space=pltpu.VMEM)
    dma = pltpu.SemaphoreType.DMA
    activated, grad_features, grad_weight = pl.pallas_call(
        functools.partial(kernel, nx, ny),
        out_shape=(
            jax.ShapeDtypeStruct((rows, channels), bf16),
            jax.ShapeDtypeStruct((rows, channels), bf16),
            jax.ShapeDtypeStruct((OFFSETS, slice_x, slice_y), f32),
        ),
        in_specs=[pl.BlockSpec(memory_space=pltpu.SMEM)] + [vmem] * 7,
        out_specs=(vmem, vmem, vmem),
        scratch_shapes=[
            pltpu.VMEM((2, 8, window, channels), bf16),
            pltpu.VMEM((2, 8, window, channels), bf16),
            pltpu.VMEM((32, rows), jnp.int32),
            pltpu.VMEM((2, block, 2 * channels), bf16),
            pltpu.VMEM((rows, OFFSETS * channels), bf16),
            pltpu.VMEM((rows, channels), bf16),
            pltpu.VMEM((rows, channels), bf16),
            pltpu.VMEM((block, 2 * channels), f32),
            pltpu.VMEM((rows, channels), f32),
            pltpu.VMEM((2, 8, window, channels), bf16),
            pltpu.VMEM((8, halo, channels), bf16),
            pltpu.VMEM((2, ny, 8, channels), f32),
            pltpu.VMEM((2, nx, 8, channels), f32),
            pltpu.VMEM((ny, slice_y, OFFSETS * channels), bf16),
            pltpu.VMEM((ny, slice_y, OFFSETS * channels), bf16),
            pltpu.VMEM((nx, groups, slice_x, channels), bf16),
            pltpu.VMEM((nx, groups, slice_x, channels), bf16),
            dma((8,)), dma((8,)),
            dma((2, ny)), dma((2, ny)),
            dma((2, nx)), dma((2, nx)),
            dma((2, 8)), dma((2, 8)),
            dma((ny,)), dma((ny,)),
            dma((nx,)), dma((nx,)),
        ],
        compiler_params=pltpu.CompilerParams(
            collective_id=0, has_side_effects=True, vmem_limit_bytes=48 * 1024 * 1024
        ),
    )(
        live_count,
        features[0, 0],
        neighbour_map[0, 0],
        send_rows[0, 0],
        weight,
        gain.reshape(1, -1),
        shift.reshape(1, -1),
        cotangent[0, 0],
    )
    return activated[None, None], grad_features[None, None], grad_weight


def solution(mesh):
    return jax.shard_map(
        per_device,
        mesh=mesh,
        in_specs=(
            P("bx", "by", None, None),
            P("bx", "by"),
            P("bx", "by", None, None),
            P("bx", "by", None, None),
            P(),
            P(),
            P(),
            P("bx", "by", None, None),
        ),
        out_specs=(P("bx", "by", None, None), P("bx", "by", None, None), P(None, "bx", "by")),
        check_vma=False,
    )
```

time: 365 us -> 75.1 us (0.21)
  blocking collectives: 124 us -> 0 us
  matrix products: 98.4 us -> 0 us
  waiting for transfers between devices: 70.5 us -> 0 us
  Pallas kernels: 0 us -> 66.8 us
  starting transfers between devices: 17.7 us -> 0 us
  between operations: 15.7 us -> 1.32 us
  other arithmetic: 13.6 us -> 0 us
  local copies, waits for them, and re-layouts: 18.3 us -> 6.74 us
  loops' own time: 5.44 us -> 0 us
    psum x3 -> x0, blocking collectives: 124 us -> none  [the longest x1 43.9 us: per_device(): lax.psum((jnp.sum(conv_float * live_mask, axis=0), local_count), ('bx', '...]
    dot_general x12 -> x0, matrix products: 98.4 us -> none  [the longest x2 57.4 us: backward_block(): jnp.einsum('kbw,bkc->wc', selector, column_grad, precision=lax.Precision....]
    pallas_call x0 -> x1, Pallas kernels: none -> 66.8 us  [per_device(): pl.pallas_call(functools.partial(kernel, nx, ny), out_shape=(jax.ShapeDty...]
    reduce_scatter x1 -> x0, waiting for transfers between devices: 41.6 us -> none  [per_device(): lax.psum_scatter(weight_terms.astype(jnp.bfloat16), 'bx', scatter_dimensi...]
    ppermute x8 -> x0, starting transfers between devices: 17.7 us -> none  [the longest x4 12.3 us: extended(): lax.ppermute(tail, axis, [(i, (i + 1) % count) for i in range(ends)])]
    unnamed x3 -> x0, waiting for transfers between devices: 16.5 us -> none
    ppermute x8 -> x0, waiting for transfers between devices: 12.4 us -> none  [the longest x4 9.83 us: extended(): lax.ppermute(head, axis, [((i + 1) % count, i) for i in range(ends)])]
    another operation x2 -> x0, loops' own time: 5.44 us -> none  [the longest x1 2.75 us: per_device(): lax.scan(backward_block, start_acc, (index_blocks, column_blocks, grad_bl...]
  transfers between devices with their start and end apart: 10 -> 0, of which waited for: 7 -> 0; matrix products, arithmetic and copies ran while one was open for 2% -> 0% of each run, Pallas kernels for 0% -> 0%
where the time goes in v1:
time: 75.1 us; the launch traced here: 74.9 us
  Pallas kernels  66.8 us (89%)
  local copies, waits for them, and re-layouts  6.74 us (9%)
  between operations  1.32 us (2%)
    pallas_call x1, Pallas kernels, per_device(): pl.pallas_call(functools.partial(kernel, nx, ny), out_shape=(jax.ShapeDty...  66.8 us
    unnamed x16, local copies, waits for them, and re-layouts  6.74 us

profile of v1, /device:TPU:0, one launch (start us, length us, event | category | flops | bytes accessed | tf_op | source)
XLA Modules:
  0.0 74.9 jit_solution(6884181460941065453)
XLA Ops:
  1.3 0.0 copy-start.3
  1.3 0.9 %copy.13 = s32[1,1,27,1024]{3,2,1,0:T(8,128)S(1)} copy(s32[1,1,27,1024]{3,1,2,0:T(1,128)} %param.10) | data formatting | bytes 221184
  2.2 0.0 copy-start.4
  2.2 0.0 copy-start.5
  2.2 0.0 copy-done.3
  2.2 0.6 copy-done.4
  2.9 0.0 copy-done.5
  2.9 0.0 copy-start
  2.9 1.2 %copy-done = bf16[3456,128]{1,0:T(8,128)(2,1)S(1)} copy-done((bf16[3456,128]{1,0:T(8,128)(2,1)S(1)}, bf16[3456,128]{1,0:T(8,128)(2,1)}, u32[]{:S(2)}) %copy-start) | copy-done | bytes 884760
  4.1 0.0 copy-start.1
  4.1 0.9 %copy-done.1 = bf16[1,1,1024,128]{3,2,1,0:T(8,128)(2,1)S(1)} copy-done((bf16[1,1,1024,128]{3,2,1,0:T(8,128)(2,1)S(1)}, bf16[1,1,1024,128]{3,2,1,0:T(8,128)(2,1)}, u32[]{:S(2)}) %copy-start.1) | copy-done | bytes 262168
  5.0 0.0 copy-start.2
  5.0 0.9 %copy-done.2 = bf16[1,1,1024,128]{3,2,1,0:T(8,128)(2,1)S(1)} copy-done((bf16[1,1,1024,128]{3,2,1,0:T(8,128)(2,1)S(1)}, bf16[1,1,1024,128]{3,2,1,0:T(8,128)(2,1)}, u32[]{:S(2)}) %copy-start.2) | copy-done | bytes 262168
  6.0 66.8 %shard_map.103 = (bf16[1024,128]{1,0:T(8,128)(2,1)S(1)}, bf16[1024,128]{1,0:T(8,128)(2,1)S(1)}, f32[27,16,32]{2,1,0:T(8,128)S(1)}) custom-call(s32[1,1]{1,0:T(1,128)S(6)} %copy.17.live_ref, bf16[1024,128]{1,0:T(8,128)(2,1)S(1)} %bitcast.11, s32[27,1024]{1,0:T(8,128)S(1)} %bitcast.10, s32[8,128]{1,0:T(8,128)S(1)} %bitcast.15, bf16[3456,128]{1,0:T(8,128)(2,1)S(1)} %copy-done, ...), custom_call_target="tpu_custom_call" | custom-call | tf_op jit(solution)/shard_map/pallas_call | solution.py:383
  72.8 0.7 copy.18
  73.5 0.7 copy.19
  74.2 0.7 copy.20
Async XLA Ops:
  1.3 1.0 %copy-start.3 = (s32[1,1,8,128]{3,2,1,0:T(8,128)S(1)}, s32[1,1,8,128]{3,2,1,0:T(8,128)}, u32[]{:S(2)}) copy-start(s32[1,1,8,128]{3,2,1,0:T(8,128)} %param.11) | copy-start | bytes 12292
  2.2 0.7 copy-start.4
  2.2 0.7 copy-start.5
  2.9 1.2 %copy-start = (bf16[3456,128]{1,0:T(8,128)(2,1)S(1)}, bf16[3456,128]{1,0:T(8,128)(2,1)}, u32[]{:S(2)}) copy-start(bf16[3456,128]{1,0:T(8,128)(2,1)} %weight.1) | copy-start | bytes 2654212
  4.1 0.9 %copy-start.1 = (bf16[1,1,1024,128]{3,2,1,0:T(8,128)(2,1)S(1)}, bf16[1,1,1024,128]{3,2,1,0:T(8,128)(2,1)}, u32[]{:S(2)}) copy-start(bf16[1,1,1024,128]{3,2,1,0:T(8,128)(2,1)} %param.8) | copy-start | bytes 786436
  5.0 0.9 %copy-start.2 = (bf16[1,1,1024,128]{3,2,1,0:T(8,128)(2,1)S(1)}, bf16[1,1,1024,128]{3,2,1,0:T(8,128)(2,1)}, u32[]{:S(2)}) copy-start(bf16[1,1,1024,128]{3,2,1,0:T(8,128)(2,1)} %param.15) | copy-start | bytes 786436

commit v2 on v1

--- a/solution.py
+++ b/solution.py
@@ -15,27 +15,46 @@
 bf16 = jnp.bfloat16
 
 
-def one_hot(mask):
-    return jnp.where(mask, 1.0, 0.0).astype(bf16)
-
-
 def lanes_from_row(row):
     return jnp.broadcast_to(row, (128, row.shape[1])).T
 
 
+def hot16(mask):
+    return jnp.where(mask, jnp.ones((), bf16), jnp.zeros((), bf16))
+
+
+def along_lanes(wide, width):
+    n = wide.shape[0]
+    wide = wide.astype(jnp.int16).reshape(n // 16, 16, 128)
+    lane = lax.broadcasted_iota(jnp.int32, (1, 16, 128), 2).astype(jnp.int16)
+    parts = [hot16(wide == lane + jnp.int16(t)).reshape(n, 128) for t in range(0, width, 128)]
+    return jnp.concatenate(parts, axis=1)
+
+
+def along_rows(row, width):
+    place = lax.broadcasted_iota(jnp.int32, (width, 128), 0).astype(jnp.int16)
+    row = jnp.broadcast_to(row, (16, row.shape[1])).astype(jnp.int16)
+    parts = []
+    for t in range(0, row.shape[1], 128):
+        piece = row[:, t : t + 128]
+        parts.append(
+            hot16(place.reshape(width // 16, 16, 128) == piece[None]).reshape(width, 128)
+        )
+    return jnp.concatenate(parts, axis=1)
+
+
 def row_selector(row, width):
-    wide = lanes_from_row(row)
-    lane = lax.broadcasted_iota(jnp.int32, wide.shape, 1)
-    return jnp.concatenate([one_hot(wide == lane + j) for j in range(0, width, 128)], axis=1)
+    return along_lanes(lanes_from_row(row), width)
 
 
 def kernel(
-    nx, ny, live_ref, feat, nmap, send, weight, gain, shift, cot,
+    nx, ny, live_ref, feat_in, nmap_in, send_in, weight_in, gain, shift, cot_in,
     act_out, gf_out, gw_out,
+    feat, nmap, send, weight, cot, picks,
     outgoing, incoming, code, table, cols, conv, grad, acc, own_tab, hbuf, returned,
     stat_y, stat_x, part, part_in, piece, piece_in,
     h_send, h_recv, sy_send, sy_recv, sx_send, sx_recv, r_send, r_recv,
-    wy_send, wy_recv, wx_send, wx_recv,
+    wy_send, wy_recv, wx_send, wx_recv, in_sems,
 ):
     x, y = lax.axis_index("bx"), lax.axis_index("by")
     rows, channels = feat.shape
@@ -56,6 +75,15 @@
 
     def near(dx, dy):
         return (x + dx, y + dy)
+
+    loads = [
+        pltpu.make_async_copy(src, dst, in_sems.at[i])
+        for i, (src, dst) in enumerate(
+            [(send_in, send), (feat_in, feat), (nmap_in, nmap), (weight_in, weight), (cot_in, cot)]
+        )
+    ]
+    for load in loads:
+        load.start()
 
     barrier = pltpu.get_barrier_semaphore()
     for d in range(1, ny):
@@ -68,6 +96,8 @@
         def _(dx=dx, dy=dy):
             pl.semaphore_signal(barrier, inc=1, device_id=near(dx, dy), device_id_type=MESH)
 
+    loads[0].wait()
+    loads[1].wait()
     for s in range(8):
         chosen = jnp.dot(
             row_selector(send[s : s + 1, :], rows), feat[...], preferred_element_type=f32
@@ -109,6 +139,7 @@
             incoming[:, s] = jnp.zeros((2, window, channels), bf16)
             returned[s] = jnp.zeros((2 * window, channels), bf16)
 
+    loads[2].wait()
     entry = nmap[...]
     beyond = entry - rows
     target = beyond // (2 * window)
@@ -119,6 +150,18 @@
     own = jnp.where(entry >= block, entry - block, entry)
     code[0:OFFSETS, :] = jnp.where(entry < rows, own, far)
 
+    def make_picks(first, last):
+        def one(k, carry):
+            for q in range(2):
+                row = jnp.bitwise_and(code[pl.ds(k, 1), q * block : (q + 1) * block], 1023)
+                at = pl.ds(pl.multiple_of(k * block, 128), block)
+                picks[q, :, at] = along_rows(row, block)
+            return carry
+
+        lax.fori_loop(first, last, one, 0)
+
+    make_picks(0, 9)
+
     for q in range(2):
         table[q, :, 0:channels] = feat[q * block : (q + 1) * block, :]
     for s, (dx, dy) in enumerate(directions):
@@ -128,6 +171,7 @@
     for q in range(2):
         table[q, :, channels:] = incoming[q].reshape(block, channels)
 
+    loads[3].wait()
     for q in range(2):
         lo = q * block
 
@@ -136,11 +180,7 @@
                 k = g * GROUP + j
                 row = code[pl.ds(k, 1), lo : lo + block]
                 wide = lanes_from_row(row)
-                low = jnp.bitwise_and(wide, 1023)
-                lane = lax.broadcasted_iota(jnp.int32, wide.shape, 1)
-                pick = jnp.concatenate(
-                    [one_hot(low == lane + t) for t in range(0, block, 128)], axis=1
-                )
+                pick = along_lanes(jnp.bitwise_and(wide, 1023), block)
                 both = jnp.dot(pick, table[q], preferred_element_type=f32)
                 got = jnp.where(wide >= 1024, both[:, channels:], both[:, :channels])
                 cols[lo : lo + block, pl.ds(pl.multiple_of(k * 128, 128), 128)] = got.astype(bf16)
@@ -151,7 +191,7 @@
             cols[lo : lo + block, :], weight[...], preferred_element_type=f32
         ).astype(bf16)
 
-    def spread(buf, r, me, count, peer, send_sems, recv_sems):
+    def spread(buf, r, me, count, peer, send_sems, recv_sems, meanwhile):
         def copy(d, arriving):
             other = lax.rem(me + d, count)
             place = other if arriving else me
@@ -166,6 +206,7 @@
 
         for d in range(1, count):
             copy(d, False).start()
+        make_picks(*meanwhile)
         for d in range(1, count):
             copy(d, True).wait_recv()
         for d in range(1, count):
@@ -199,13 +240,14 @@
     dev = (values - s_own / n_own) * live
     m2_own = jnp.sum(dev * dev, axis=0, keepdims=True)
     put(stat_y, 0, y, n_own, s_own, m2_own)
-    spread(stat_y, 0, y, ny, along_y, sy_send, sy_recv)
+    spread(stat_y, 0, y, ny, along_y, sy_send, sy_recv, (9, 13))
     put(stat_x, 0, x, *pooled(stat_y, 0, ny))
-    spread(stat_x, 0, x, nx, along_x, sx_send, sx_recv)
+    spread(stat_x, 0, x, nx, along_x, sx_send, sx_recv, (13, 18))
     total, s_all, m2_all = pooled(stat_x, 0, nx)
     center = s_all / total
     inverse = lax.rsqrt(m2_all / total + epsilon)
 
+    loads[4].wait()
     normalized = (values - center) * inverse
     before = gain[...] * normalized + shift[...]
     act_out[...] = (jnp.maximum(before, 0.0) * live).astype(bf16)
@@ -215,9 +257,9 @@
         jnp.sum(upstream, axis=0, keepdims=True),
         jnp.sum(upstream * normalized, axis=0, keepdims=True),
     )
-    spread(stat_y, 1, y, ny, along_y, sy_send, sy_recv)
+    spread(stat_y, 1, y, ny, along_y, sy_send, sy_recv, (18, 22))
     stat_x[1, x] = functools.reduce(jnp.add, [stat_y[1, i] for i in range(ny)])
-    spread(stat_x, 1, x, nx, along_x, sx_send, sx_recv)
+    spread(stat_x, 1, x, nx, along_x, sx_send, sx_recv, (22, 27))
     sums = functools.reduce(jnp.add, [stat_x[1, i] for i in range(nx)])
     sum_up, sum_cross = sums[0:1], sums[1:2]
     conv_grad = (
@@ -261,11 +303,10 @@
                 grad[lo : lo + block, :], weight[at, :], (((1,), (1,)), ((), ())),
                 preferred_element_type=f32,
             )
-            picks, terms = [], []
-            place = lax.broadcasted_iota(jnp.int32, (block, block), 0)
+            terms = []
+            chosen_at = pl.ds(pl.multiple_of(g * GROUP * block, 128), GROUP * block)
             for j in range(GROUP):
                 row = code[pl.ds(g * GROUP + j, 1), lo : lo + block]
-                picks.append(one_hot(place == jnp.bitwise_and(row, 1023)))
                 away = lanes_from_row(row) >= 1024
                 term = col_grad[:, j * 128 : (j + 1) * 128]
                 terms.append(
@@ -274,7 +315,7 @@
                     ).astype(bf16)
                 )
             acc[...] += jnp.dot(
-                jnp.concatenate(picks, axis=1),
+                picks[q, :, chosen_at],
                 jnp.concatenate(terms, axis=0),
                 preferred_element_type=f32,
             )
@@ -352,8 +393,7 @@
             @pl.when(exists(dx, dy))
             def _(q=q, s=s):
                 back_copy(q, s, True).wait_recv()
-    place = lax.broadcasted_iota(jnp.int32, (rows, 2 * window), 0)
-    pick = jnp.concatenate([one_hot(place == send[s : s + 1, :]) for s in range(8)], axis=1)
+    pick = jnp.concatenate([along_rows(send[s : s + 1, :], rows) for s in range(8)], axis=1)
     added = jnp.dot(
         pick, returned[...].reshape(8 * 2 * window, channels), preferred_element_type=f32
     )
@@ -379,6 +419,7 @@
     slice_x, slice_y = channels // nx, channels // ny
     groups = -(-OFFSETS // ny)
     vmem = pl.BlockSpec(memory_space=pltpu.VMEM)
+    hbm = pl.BlockSpec(memory_space=pltpu.HBM)
     dma = pltpu.SemaphoreType.DMA
     activated, grad_features, grad_weight = pl.pallas_call(
         functools.partial(kernel, nx, ny),
@@ -387,9 +428,17 @@
             jax.ShapeDtypeStruct((rows, channels), bf16),
             jax.ShapeDtypeStruct((OFFSETS, slice_x, slice_y), f32),
         ),
-        in_specs=[pl.BlockSpec(memory_space=pltpu.SMEM)] + [vmem] * 7,
+        in_specs=[
+            pl.BlockSpec(memory_space=pltpu.SMEM), hbm, hbm, hbm, hbm, vmem, vmem, hbm,
+        ],
         out_specs=(vmem, vmem, vmem),
         scratch_shapes=[
+            pltpu.VMEM((rows, channels), bf16),
+            pltpu.VMEM((OFFSETS, rows), jnp.int32),
+            pltpu.VMEM((8, halo), jnp.int32),
+            pltpu.VMEM((OFFSETS * channels, channels), bf16),
+            pltpu.VMEM((rows, channels), bf16),
+            pltpu.VMEM((2, block, OFFSETS * block), bf16),
             pltpu.VMEM((2, 8, window, channels), bf16),
             pltpu.VMEM((2, 8, window, channels), bf16),
             pltpu.VMEM((32, rows), jnp.int32),
@@ -413,9 +462,10 @@
             dma((2, 8)), dma((2, 8)),
             dma((ny,)), dma((ny,)),
             dma((nx,)), dma((nx,)),
+            dma((5,)),
         ],
         compiler_params=pltpu.CompilerParams(
-            collective_id=0, has_side_effects=True, vmem_limit_bytes=48 * 1024 * 1024
+            collective_id=0, has_side_effects=True, vmem_limit_bytes=58 * 1024 * 1024
         ),
     )(
         live_count,

time: 75.1 us -> 73.1 us (0.973)
  local copies, waits for them, and re-layouts: 6.74 us -> 5.01 us
    unnamed x16 -> x8, local copies, waits for them, and re-layouts: 6.74 us -> 5.01 us
where the time goes in v2:
time: 73.1 us; the launch traced here: 72.8 us
  Pallas kernels  66.5 us (91%)
  local copies, waits for them, and re-layouts  5.01 us (7%)
  between operations  1.3 us (2%)
    pallas_call x1, Pallas kernels, per_device(): pl.pallas_call(functools.partial(kernel, nx, ny), out_shape=(jax.ShapeDty...  66.5 us
    unnamed x8, local copies, waits for them, and re-layouts  5.01 us

profile of v2, /device:TPU:0, one launch (start us, length us, event | category | flops | bytes accessed | tf_op | source)
XLA Modules:
  0.0 72.8 jit_solution(15613798599473490771)
XLA Ops:
  1.3 1.6 %copy.13 = s32[1,1,27,1024]{3,2,1,0:T(8,128)} copy(s32[1,1,27,1024]{3,1,2,0:T(1,128)} %param.10) | data formatting | bytes 221184
  2.9 66.5 %shard_map.103 = (bf16[1024,128]{1,0:T(8,128)(2,1)}, bf16[1024,128]{1,0:T(8,128)(2,1)}, f32[27,16,32]{2,1,0:T(8,128)}) custom-call(s32[1,1]{1,0:T(1,128)S(6)} %copy.17.live_ref, bf16[1024,128]{1,0:T(8,128)(2,1)} %bitcast.11, s32[27,1024]{1,0:T(8,128)} %bitcast.10, s32[8,128]{1,0:T(8,128)} %bitcast.15, bf16[3456,128]{1,0:T(8,128)(2,1)} %weight_in.1, ...), custom_call_target="tpu_custom_call" | custom-call | tf_op jit(solution)/shard_map/pallas_call | solution.py:424
  69.4 0.0 copy-start
  69.4 1.7 %copy.18 = bf16[1,1,1024,128]{3,2,1,0:T(8,128)(2,1)} copy(bf16[1,1,1024,128]{3,2,1,0:T(8,128)(2,1)} %bitcast.14) | data formatting | bytes 524288
  71.1 0.0 copy-done
  71.1 0.0 copy-start.1
  71.1 0.7 copy.19
  71.8 0.3 copy-done.1
  72.1 0.7 copy.20
Async XLA Ops:
  69.4 1.7 %copy-start = (bf16[1024,128]{1,0:T(8,128)(2,1)S(1)}, bf16[1024,128]{1,0:T(8,128)(2,1)}, u32[]{:S(2)}) copy-start(bf16[1024,128]{1,0:T(8,128)(2,1)} %get-tuple-element.7) | copy-start | bytes 786436
  71.1 1.0 %copy-start.1 = (f32[27,16,32]{2,1,0:T(8,128)S(1)}, f32[27,16,32]{2,1,0:T(8,128)}, u32[]{:S(2)}) copy-start(f32[27,16,32]{2,1,0:T(8,128)} %get-tuple-element.14) | copy-start | bytes 165892

commit v3 on v2

--- a/solution.py
+++ b/solution.py
@@ -10,6 +10,7 @@
 epsilon = 1e-05
 OFFSETS = 27
 GROUP = 3
+WIDE_GROUP = 9
 MESH = pl.DeviceIdType.MESH
 f32 = jnp.float32
 bf16 = jnp.bfloat16
@@ -51,10 +52,10 @@
     nx, ny, live_ref, feat_in, nmap_in, send_in, weight_in, gain, shift, cot_in,
     act_out, gf_out, gw_out,
     feat, nmap, send, weight, cot, picks,
-    outgoing, incoming, code, table, cols, conv, grad, acc, own_tab, hbuf, returned,
-    stat_y, stat_x, part, part_in, piece, piece_in,
+    outgoing, incoming, code, code_t, table, cols, conv, grad, acc, own_tab, hbuf, returned,
+    stat_y, stat_x, part, mate_in, pair_out, part_in, piece, piece_in,
     h_send, h_recv, sy_send, sy_recv, sx_send, sx_recv, r_send, r_recv,
-    wy_send, wy_recv, wx_send, wx_recv, in_sems,
+    wm_send, wm_recv, wy_send, wy_recv, wx_send, wx_recv, in_sems,
 ):
     x, y = lax.axis_index("bx"), lax.axis_index("by")
     rows, channels = feat.shape
@@ -148,7 +149,16 @@
     slot = jnp.where(target > 4, target - 1, target)
     far = jnp.where(target == 4, 1023, 1024 + slot * window + inside)
     own = jnp.where(entry >= block, entry - block, entry)
-    code[0:OFFSETS, :] = jnp.where(entry < rows, own, far)
+    coded = jnp.where(entry < rows, own, far)
+    coded = coded.reshape(OFFSETS, rows // 128, 128)
+    for i in range(rows // 128):
+        code[0:OFFSETS, i * 128 : (i + 1) * 128] = coded[:, i, :]
+    code[OFFSETS:, :] = jnp.zeros((32 - OFFSETS, rows), jnp.int32)
+    code_t[...] = jnp.concatenate([code[...], jnp.zeros((96, rows), jnp.int32)], axis=0).T
+
+    def columns_from(lo, first):
+        turn = lax.rem(128 - first, 128)
+        return pltpu.roll(code_t[lo : lo + block, :], turn, axis=1)
 
     def make_picks(first, last):
         def one(k, carry):
@@ -176,17 +186,17 @@
         lo = q * block
 
         def gather(g, carry):
-            for j in range(GROUP):
-                k = g * GROUP + j
-                row = code[pl.ds(k, 1), lo : lo + block]
-                wide = lanes_from_row(row)
+            turned = columns_from(lo, g * WIDE_GROUP)
+            for j in range(WIDE_GROUP):
+                k = g * WIDE_GROUP + j
+                wide = jnp.broadcast_to(turned[:, j : j + 1], (block, 128))
                 pick = along_lanes(jnp.bitwise_and(wide, 1023), block)
                 both = jnp.dot(pick, table[q], preferred_element_type=f32)
                 got = jnp.where(wide >= 1024, both[:, channels:], both[:, :channels])
                 cols[lo : lo + block, pl.ds(pl.multiple_of(k * 128, 128), 128)] = got.astype(bf16)
             return carry
 
-        lax.fori_loop(0, OFFSETS // GROUP, gather, 0)
+        lax.fori_loop(0, OFFSETS // WIDE_GROUP, gather, 0)
         conv[lo : lo + block, :] = jnp.dot(
             cols[lo : lo + block, :], weight[...], preferred_element_type=f32
         ).astype(bf16)
@@ -273,29 +283,47 @@
     def weight_part(g, carry):
         at = pl.ds(pl.multiple_of(g * wide_part, 128), wide_part)
         term = jnp.dot(flipped, cols[:, at], preferred_element_type=f32).astype(bf16)
-        part[:, :, at] = term.reshape(ny, slice_y, wide_part)
+        term = term.reshape(ny, slice_y, wide_part)
+        for i in range(ny):
+            part[i % 2, i // 2, :, at] = term[i]
         return carry
 
     lax.fori_loop(0, OFFSETS // GROUP, weight_part, 0)
 
-    def part_copy(d, arriving):
-        other = lax.rem(y + d, ny)
-        place = other if arriving else y
+    half = ny // 2
+    mine, pair = lax.rem(y, 2), y // 2
+    mate = y + 1 - 2 * mine
+
+    def mate_copy():
         return pltpu.make_async_remote_copy(
-            src_ref=part.at[other],
+            src_ref=part.at[1 - mine],
+            dst_ref=mate_in,
+            send_sem=wm_send.at[0],
+            recv_sem=wm_recv.at[0],
+            device_id=(x, mate),
+            device_id_type=MESH,
+        )
+
+    mate_copy().start()
+
+    def pair_copy(d, arriving):
+        other = lax.rem(pair + d, half)
+        place = other if arriving else pair
+        return pltpu.make_async_remote_copy(
+            src_ref=pair_out.at[other],
             dst_ref=part_in.at[place],
             send_sem=wy_send.at[other],
             recv_sem=wy_recv.at[place],
-            device_id=(x, other),
+            device_id=(x, 2 * other + mine),
             device_id_type=MESH,
         )
 
-    for d in range(1, ny):
-        part_copy(d, False).start()
-
-    def scatter(q):
+    steps = OFFSETS // GROUP
+
+    def scatter(q, first, last):
         lo = q * block
-        acc[...] = jnp.zeros_like(acc)
+        if first == 0:
+            acc[...] = jnp.zeros_like(acc)
 
         def step(g, carry):
             at = pl.ds(pl.multiple_of(g * wide_part, 128), wide_part)
@@ -304,10 +332,10 @@
                 preferred_element_type=f32,
             )
             terms = []
+            turned = columns_from(lo, g * GROUP)
             chosen_at = pl.ds(pl.multiple_of(g * GROUP * block, 128), GROUP * block)
             for j in range(GROUP):
-                row = code[pl.ds(g * GROUP + j, 1), lo : lo + block]
-                away = lanes_from_row(row) >= 1024
+                away = jnp.broadcast_to(turned[:, j : j + 1], (block, 128)) >= 1024
                 term = col_grad[:, j * 128 : (j + 1) * 128]
                 terms.append(
                     jnp.concatenate(
@@ -321,7 +349,9 @@
             )
             return carry
 
-        lax.fori_loop(0, OFFSETS // GROUP, step, 0)
+        lax.fori_loop(first, last, step, 0)
+        if last < steps:
+            return
         own_tab[lo : lo + block, :] = acc[:, 0:channels]
         hbuf[q] = acc[:, channels:].astype(bf16).reshape(8, window, channels)
 
@@ -342,12 +372,18 @@
             def _(s=s):
                 back_copy(q, s, False).start()
 
-    scatter(0)
+    scatter(0, 0, 3)
+    mate_copy().wait_recv()
+    pair_out[...] = (part[mine].astype(f32) + mate_in[...].astype(f32)).astype(bf16)
+    for d in range(1, half):
+        pair_copy(d, False).start()
+    scatter(0, 3, steps)
     send_back(0)
-
-    part_in[y] = part[y]
-    for d in range(1, ny):
-        part_copy(d, True).wait_recv()
+    scatter(1, 0, 2)
+
+    part_in[pair] = pair_out[pair]
+    for d in range(1, half):
+        pair_copy(d, True).wait_recv()
     for g in range(groups):
         strips = []
         for j in range(ny):
@@ -375,7 +411,7 @@
     for d in range(1, nx):
         piece_copy(d, False).start()
 
-    scatter(1)
+    scatter(1, 2, steps)
     send_back(1)
 
     piece_in[x] = piece[x]
@@ -405,8 +441,9 @@
             halo_copy(s).wait_send()
             for q in range(2):
                 back_copy(q, s, False).wait_send()
-    for d in range(1, ny):
-        part_copy(d, False).wait_send()
+    mate_copy().wait_send()
+    for d in range(1, half):
+        pair_copy(d, False).wait_send()
     for d in range(1, nx):
         piece_copy(d, False).wait_send()
 
@@ -434,7 +471,7 @@
         out_specs=(vmem, vmem, vmem),
         scratch_shapes=[
             pltpu.VMEM((rows, channels), bf16),
-            pltpu.VMEM((OFFSETS, rows), jnp.int32),
+            pltpu.VMEM((OFFSETS * rows // 128, 128), jnp.int32),
             pltpu.VMEM((8, halo), jnp.int32),
             pltpu.VMEM((OFFSETS * channels, channels), bf16),
             pltpu.VMEM((rows, channels), bf16),
@@ -442,6 +479,7 @@
             pltpu.VMEM((2, 8, window, channels), bf16),
             pltpu.VMEM((2, 8, window, channels), bf16),
             pltpu.VMEM((32, rows), jnp.int32),
+            pltpu.VMEM((rows, 128), jnp.int32),
             pltpu.VMEM((2, block, 2 * channels), bf16),
             pltpu.VMEM((rows, OFFSETS * channels), bf16),
             pltpu.VMEM((rows, channels), bf16),
@@ -452,25 +490,28 @@
             pltpu.VMEM((8, halo, channels), bf16),
             pltpu.VMEM((2, ny, 8, channels), f32),
             pltpu.VMEM((2, nx, 8, channels), f32),
-            pltpu.VMEM((ny, slice_y, OFFSETS * channels), bf16),
-            pltpu.VMEM((ny, slice_y, OFFSETS * channels), bf16),
+            pltpu.VMEM((2, ny // 2, slice_y, OFFSETS * channels), bf16),
+            pltpu.VMEM((ny // 2, slice_y, OFFSETS * channels), bf16),
+            pltpu.VMEM((ny // 2, slice_y, OFFSETS * channels), bf16),
+            pltpu.VMEM((ny // 2, slice_y, OFFSETS * channels), bf16),
             pltpu.VMEM((nx, groups, slice_x, channels), bf16),
             pltpu.VMEM((nx, groups, slice_x, channels), bf16),
             dma((8,)), dma((8,)),
             dma((2, ny)), dma((2, ny)),
             dma((2, nx)), dma((2, nx)),
             dma((2, 8)), dma((2, 8)),
-            dma((ny,)), dma((ny,)),
+            dma((1,)), dma((1,)),
+            dma((ny // 2,)), dma((ny // 2,)),
             dma((nx,)), dma((nx,)),
             dma((5,)),
         ],
         compiler_params=pltpu.CompilerParams(
-            collective_id=0, has_side_effects=True, vmem_limit_bytes=58 * 1024 * 1024
+            collective_id=0, has_side_effects=True, vmem_limit_bytes=52 * 1024 * 1024
         ),
     )(
         live_count,
         features[0, 0],
-        neighbour_map[0, 0],
+        neighbour_map.reshape(-1, 128),
         send_rows[0, 0],
         weight,
         gain.reshape(1, -1),

time: 73.1 us -> 68.4 us (0.936); the launches traced: 72.8 us -> 67.3 us
  Pallas kernels: 66.5 us -> 60.4 us
    pallas_call x1, Pallas kernels: 66.5 us -> 60.4 us  [per_device(): pl.pallas_call(functools.partial(kernel, nx, ny), out_shape=(jax.ShapeDty...]
    unnamed x8 -> x15, local copies, waits for them, and re-layouts: 5.01 us -> 5.56 us
where the time goes in v3:
time: 68.4 us; the launch traced here: 67.3 us
  Pallas kernels  60.4 us (88%)
  local copies, waits for them, and re-layouts  5.56 us (8%)
  between operations  1.32 us (2%)
    pallas_call x1, Pallas kernels, per_device(): pl.pallas_call(functools.partial(kernel, nx, ny), out_shape=(jax.ShapeDty...  60.4 us
    unnamed x15, local copies, waits for them, and re-layouts  5.56 us

profile of v3, /device:TPU:0, one launch (start us, length us, event | category | flops | bytes accessed | tf_op | source)
XLA Modules:
  0.0 67.3 jit_solution(10917285564575856510)
XLA Ops:
  1.3 0.0 copy-start.3
  1.3 0.0 copy-start.4
  1.3 0.0 copy-start.5
  1.3 0.7 copy-done.3
  2.0 0.0 copy-done.4
  2.0 0.0 copy-done.5
  2.0 0.0 copy-start
  2.0 0.9 %copy-done = bf16[1,1,1024,128]{3,2,1,0:T(8,128)(2,1)S(1)} copy-done((bf16[1,1,1024,128]{3,2,1,0:T(8,128)(2,1)S(1)}, bf16[1,1,1024,128]{3,2,1,0:T(8,128)(2,1)}, u32[]{:S(2)}) %copy-start) | copy-done | bytes 262168
  2.9 0.0 copy-start.1
  2.9 0.9 %copy-done.1 = bf16[1,1,1024,128]{3,2,1,0:T(8,128)(2,1)S(1)} copy-done((bf16[1,1,1024,128]{3,2,1,0:T(8,128)(2,1)S(1)}, bf16[1,1,1024,128]{3,2,1,0:T(8,128)(2,1)}, u32[]{:S(2)}) %copy-start.1) | copy-done | bytes 262168
  3.9 0.0 copy-start.2
  3.9 0.9 %copy-done.2 = s32[1,1,27,1024]{3,1,2,0:T(1,128)S(1)} copy-done((s32[1,1,27,1024]{3,1,2,0:T(1,128)S(1)}, s32[1,1,27,1024]{3,1,2,0:T(1,128)}, u32[]{:S(2)}) %copy-start.2) | copy-done | bytes 110616
  4.8 60.4 %shard_map.103 = (bf16[1024,128]{1,0:T(8,128)(2,1)S(1)}, bf16[1024,128]{1,0:T(8,128)(2,1)S(1)}, f32[27,16,32]{2,1,0:T(8,128)S(1)}) custom-call(s32[1,1]{1,0:T(1,128)S(6)} %copy.14.live_ref, bf16[1024,128]{1,0:T(8,128)(2,1)S(1)} %bitcast.8, s32[216,128]{1,0:T(8,128)S(1)} %bitcast.12, s32[8,128]{1,0:T(8,128)S(1)} %bitcast.13, bf16[3456,128]{1,0:T(8,128)(2,1)} %weight_in.1, ...), custom_call_target="tpu_custom_call" | custom-call | tf_op jit(solution)/shard_map/pallas_call | solution.py:461
  65.2 0.7 %copy.15 = bf16[1,1,1024,128]{3,2,1,0:T(8,128)(2,1)} copy(bf16[1,1,1024,128]{3,2,1,0:T(8,128)(2,1)S(1)} %bitcast.11) | data formatting | bytes 524288
  65.9 0.7 %copy.16 = bf16[1,1,1024,128]{3,2,1,0:T(8,128)(2,1)} copy(bf16[1,1,1024,128]{3,2,1,0:T(8,128)(2,1)S(1)} %bitcast.10) | data formatting | bytes 524288
  66.6 0.7 %copy.17 = f32[27,16,32]{2,1,0:T(8,128)} copy(f32[27,16,32]{2,1,0:T(8,128)S(1)} %get-tuple-element.14) | data formatting | bytes 110592
Async XLA Ops:
  1.3 0.7 %copy-start.3 = (s32[1,1,8,128]{3,2,1,0:T(8,128)S(1)}, s32[1,1,8,128]{3,2,1,0:T(8,128)}, u32[]{:S(2)}) copy-start(s32[1,1,8,128]{3,2,1,0:T(8,128)} %param.11) | copy-start | bytes 12292
  1.3 0.7 %copy-start.4 = (f32[128]{0:T(128)S(1)}, f32[128]{0:T(128)}, u32[]{:S(2)}) copy-start(f32[128]{0:T(128)} %param.13) | copy-start | bytes 1540
  1.3 0.7 %copy-start.5 = (f32[128]{0:T(128)S(1)}, f32[128]{0:T(128)}, u32[]{:S(2)}) copy-start(f32[128]{0:T(128)} %param.14) | copy-start | bytes 1540
  2.0 1.0 %copy-start = (bf16[1,1,1024,128]{3,2,1,0:T(8,128)(2,1)S(1)}, bf16[1,1,1024,128]{3,2,1,0:T(8,128)(2,1)}, u32[]{:S(2)}) copy-start(bf16[1,1,1024,128]{3,2,1,0:T(8,128)(2,1)} %param.8) | copy-start | bytes 786436
  2.9 0.9 %copy-start.1 = (bf16[1,1,1024,128]{3,2,1,0:T(8,128)(2,1)S(1)}, bf16[1,1,1024,128]{3,2,1,0:T(8,128)(2,1)}, u32[]{:S(2)}) copy-start(bf16[1,1,1024,128]{3,2,1,0:T(8,128)(2,1)} %param.15) | copy-start | bytes 786436
  3.9 0.9 %copy-start.2 = (s32[1,1,27,1024]{3,1,2,0:T(1,128)S(1)}, s32[1,1,27,1024]{3,1,2,0:T(1,128)}, u32[]{:S(2)}) copy-start(s32[1,1,27,1024]{3,1,2,0:T(1,128)} %param.10) | copy-start | bytes 331780
